TPU v7x, 32 devices: a whole 2x2x4 slice. The times are simulated.
32 devices in a mesh: dp: 4 (over x, core), grid: 8 (over z, y).
Axes of the slice: x: 2, y: 2, z: 4, core: 2. Of those that a mesh axis runs over, the one named last changes fastest.
Arguments:
- q_row: bfloat16 [8, 96, 96, 1536], P('dp', 'grid'), may hold values from -8 to 8, as said below
- k_row: bfloat16 [8, 96, 96, 1536], P('dp', 'grid'), may hold values from -8 to 8
- v_row: bfloat16 [8, 96, 96, 1536], P('dp', 'grid'), may hold values from -6 to 6
- q_col: bfloat16 [8, 96, 96, 1536], P('dp', None, 'grid'), may hold values from -8 to 8, as said below
- k_col: bfloat16 [8, 96, 96, 1536], P('dp', None, 'grid'), may hold values from -8 to 8
- cotangent: bfloat16 [8, 96, 96, 1536], P('dp', None, 'grid'), may hold values from -6 to 6
- w_value: bfloat16 [1536, 1536], P(('dp', 'grid')), may hold values from -0.15625 to 0.15625
- row_positions: int32 [96], replicated, may hold values from 0 to 95, each once
- col_positions: int32 [96], replicated, may hold values from 0 to 95, each once
- mlp_in: float32 [512], P('grid'), may hold values from -8 to 8
- mlp_bias: float32 [512], P('grid'), may hold values from -4 to 4
- mlp_out: float32 [512, 48], P('grid'), may hold values from -0.08 to 0.08
Outputs:
- attended: bfloat16 [8, 96, 96, 1536], P('dp', None, 'grid')
- grad_mlp_in: float32 [512], P('grid')
- grad_mlp_bias: float32 [512], P('grid')
- grad_mlp_out: float32 [512, 48], P('grid')
Inputs may be any that keep to these rules, and one draw needn't show every extreme that they name: q_row and k_row lie within the range. q_col and k_col lie within the range. `row_positions`: each of 0 to 95 appears once. `col_positions`: each of 0 to 95 appears once.
All inputs are finite; a program needn't handle non-finite values.
Results may differ from a plain program's by a relative error of at most 0.007.
Values may be sent and summed in bfloat16 or wider, within the bound.
A program may use at most 384 MiB of HBM per device.

v0:
```python
import jax
import jax.numpy as jnp
from jax import lax
from jax.sharding import PartitionSpec as P

G = 96
D = 1536
NH = 48
HD = 32
NOFF = 191


PRECISE = lax.Precision.HIGHEST


def offset_coords():
    delta = jnp.arange(NOFF, dtype=jnp.float32) - (G - 1)
    scaled = delta * (8.0 / (G - 1))
    return jnp.sign(scaled) * jnp.log2(jnp.abs(scaled) + 1.0) / 3.0


def offset_one_hot(positions):
    spread = positions[:, None] - positions[None, :] + (G - 1)
    levels = jnp.arange(NOFF, dtype=jnp.int32)
    return (spread.reshape(-1)[:, None] == levels[None, :]).astype(jnp.float32)


def expand_bias(one_hot, bias_table):
    flat_bias = jnp.dot(one_hot, bias_table, precision=PRECISE)
    return flat_bias.reshape(G, G, NH).transpose(2, 0, 1)


def fold_bias(one_hot, bias_grad):
    flat_grad = bias_grad.transpose(1, 2, 0).reshape(G * G, NH)
    return lax.dot_general(one_hot, flat_grad, (((0,), (0,)), ((), ())), precision=PRECISE)


def soft_grad(attn_probs, d_probs):
    return attn_probs * (d_probs - jnp.sum(attn_probs * d_probs, axis=-1, keepdims=True))


def fetch_weight(w_value):
    return lax.all_gather(w_value, ("dp", "grid"), axis=0, tiled=True)


def shards(
    q_row,
    k_row,
    v_row,
    q_col,
    k_col,
    cotangent,
    w_value,
    row_positions,
    col_positions,
    mlp_in,
    mlp_bias,
    mlp_out,
):
    images = q_row.shape[0]
    row_count = q_row.shape[1]
    col_count = q_col.shape[2]
    coords = offset_coords()
    pre_act = coords[:, None] * mlp_in[None, :] + mlp_bias[None, :]
    hidden_units = jnp.maximum(pre_act, 0.0)
    partial_table = jnp.dot(hidden_units, mlp_out, precision=PRECISE)
    table_pre = lax.psum(partial_table, "grid")
    squashed = jax.nn.sigmoid(table_pre)
    bias_table = 16.0 * squashed
    hot_cols = offset_one_hot(col_positions)
    hot_rows = offset_one_hot(row_positions)
    bias_row = expand_bias(hot_cols, bias_table)
    bias_col = expand_bias(hot_rows, bias_table)
    score_scale = HD ** (-0.5)
    query_rows = q_row.reshape(images * row_count, G, NH, HD)
    key_rows = k_row.reshape(images * row_count, G, NH, HD)
    value_rows = v_row.reshape(images * row_count, G, NH, HD)
    scores = (
        jnp.einsum("nqhd,nkhd->nhqk", query_rows, key_rows, preferred_element_type=jnp.float32)
        * score_scale
        + bias_row[None]
    )
    p_row = jax.nn.softmax(scores, axis=-1)
    p_row_b = p_row.astype(jnp.bfloat16)
    row_out = jnp.einsum(
        "nhqk,nkhd->nqhd", p_row_b, value_rows, preferred_element_type=jnp.float32
    ).astype(jnp.bfloat16)
    flat_out = row_out.reshape(images * row_count * G, D)
    whole_weight = fetch_weight(w_value)
    projected = jnp.dot(flat_out, whole_weight, preferred_element_type=jnp.float32)
    values = projected.astype(jnp.bfloat16).reshape(images, row_count, G, D)
    col_values = lax.all_to_all(values, "grid", split_axis=2, concat_axis=1, tiled=True)
    query_cols = q_col.reshape(images, G, col_count, NH, HD)
    key_cols = k_col.reshape(images, G, col_count, NH, HD)
    value_cols = col_values.reshape(images, G, col_count, NH, HD)
    scores_col = (
        jnp.einsum("bqchd,bkchd->bchqk", query_cols, key_cols, preferred_element_type=jnp.float32)
        * score_scale
        + bias_col
    )
    p_col = jax.nn.softmax(scores_col, axis=-1)
    p_col_b = p_col.astype(jnp.bfloat16)
    attended = (
        jnp.einsum("bchqk,bkchd->bqchd", p_col_b, value_cols, preferred_element_type=jnp.float32)
        .astype(jnp.bfloat16)
        .reshape(images, G, col_count, D)
    )
    grad_cols = cotangent.reshape(images, G, col_count, NH, HD)
    dprob_col = jnp.einsum(
        "bqchd,bkchd->bchqk", grad_cols, value_cols, preferred_element_type=jnp.float32
    )
    ds_col = soft_grad(p_col, dprob_col)
    col_table = fold_bias(hot_rows, jnp.sum(ds_col, axis=(0, 1)))
    col_summed = lax.psum(col_table, ("dp", "grid"))
    d_values = (
        jnp.einsum("bchqk,bqchd->bkchd", p_col_b, grad_cols, preferred_element_type=jnp.float32)
        .astype(jnp.bfloat16)
        .reshape(images, G, col_count, D)
    )
    d_rows = lax.all_to_all(d_values, "grid", split_axis=1, concat_axis=2, tiled=True)
    flat_grad = d_rows.reshape(images * row_count * G, D)
    d_flat = lax.dot_general(
        flat_grad, whole_weight, (((1,), (1,)), ((), ())), preferred_element_type=jnp.float32
    )
    d_row_out = d_flat.astype(jnp.bfloat16).reshape(images * row_count, G, NH, HD)
    dprob_row = jnp.einsum(
        "nqhd,nkhd->nhqk", d_row_out, value_rows, preferred_element_type=jnp.float32
    )
    ds_row = soft_grad(p_row, dprob_row)
    row_table = fold_bias(hot_cols, jnp.sum(ds_row, axis=0))
    table_sum = col_summed + lax.psum(row_table, ("dp", "grid"))
    batch_size = lax.axis_size("dp") * images
    table_grad = table_sum / (batch_size * G)
    pre_grad = table_grad * 16.0 * squashed * (1.0 - squashed)
    grad_mlp_out = lax.dot_general(
        hidden_units, pre_grad, (((0,), (0,)), ((), ())), precision=PRECISE
    )
    back_units = lax.dot_general(pre_grad, mlp_out, (((1,), (1,)), ((), ())), precision=PRECISE)
    unit_grad = jnp.where(pre_act > 0, back_units, 0.0)
    grad_mlp_in = jnp.sum(unit_grad * coords[:, None], axis=0)
    grad_mlp_bias = jnp.sum(unit_grad, axis=0)
    return (attended, grad_mlp_in, grad_mlp_bias, grad_mlp_out)


def solution(mesh):
    return jax.shard_map(
        shards,
        mesh=mesh,
        in_specs=(
            P("dp", "grid", None, None),
            P("dp", "grid", None, None),
            P("dp", "grid", None, None),
            P("dp", None, "grid", None),
            P("dp", None, "grid", None),
            P("dp", None, "grid", None),
            P(("dp", "grid"), None),
            P(),
            P(),
            P("grid"),
            P("grid"),
            P("grid", None),
        ),
        out_specs=(P("dp", None, "grid", None), P("grid"), P("grid"), P("grid", None)),
        check_vma=False,
    )
```

profile of v0, /device:TPU:0, one launch (start us, length us, event | category | flops | bytes accessed | tf_op | source)
XLA Modules:
  0.0 811.5 jit_solution(9014398851004224088)
XLA Ops:
  8.8 39.3 %psum.21 = f32[191,48]{0,1:T(8,128)S(1)} all-reduce(f32[191,48]{0,1:T(8,128)S(1)} %fusion.51), channel_id=1, replica_groups=mesh['dp'=4,'grid'=8] {'grid'}, use_global_device_ids=true, to_apply=%region_0.0 | all-reduce | flops 9168 | bytes 73344 | tf_op jit(solution)/shard_map/psum | solution.py:67
  81.0 11.5 %copy.137 = bf16[2,96,12,1536]{1,3,2,0:T(8,128)(2,1)} copy(bf16[2,96,12,1536]{3,1,2,0:T(8,128)(2,1)} %param.17) | data formatting | bytes 14155776 | tf_op args[5]
  92.5 31.3 %fusion.79 = (f32[2,12,48,96]{3,2,1,0:T(8,128)S(1)}, f32[2,12,48,96,96]{3,4,2,1,0:T(8,128)}) fusion(f32[48,96,96]{1,2,0:T(8,128)S(1)} %bitcast.91, bf16[2,96,12,48,32]{1,4,3,2,0:T(8,128)(2,1)} %bitcast.85, bf16[2,96,12,48,32]{1,4,3,2,0:T(8,128)(2,1)} %bitcast.84), kind=kOutput, calls=%fused_computation.89 | convolution fusion | flops 721944640 | bytes 58834944 | tf_op jit(solution)/shard_map/sub | solution.py:101
  123.8 37.6 %fusion.37 = bf16[2,12,48,96,32]{3,4,2,1,0:T(8,128)(2,1)} fusion(bf16[2,96,12,48,32]{1,4,3,2,0:T(8,128)(2,1)} %bitcast.78, f32[2,12,48,96,96]{3,4,2,1,0:T(8,128)} %get-tuple-element.33, f32[2,12,48,96]{3,2,1,0:T(8,128)S(1)} %get-tuple-element.32), kind=kOutput, calls=%fused_computation.45 | convolution fusion | flops 704249856 | bytes 57065472 | tf_op jit(solution)/shard_map/bchqk,bqchd->bkchd/dot_general | solution.py:116
  161.5 17.2 %copy.141 = bf16[2,96,12,1536]{3,0,2,1:T(2,128)(2,1)} copy(bf16[2,96,12,1536]{1,3,2,0:T(8,128)(2,1)} %bitcast.89) | data formatting | bytes 14155776 | tf_op jit(solution)/shard_map/reshape | solution.py:118
  216.6 11.5 %copy.126 = bf16[2,12,96,1536]{2,3,1,0:T(8,128)(2,1)} copy(bf16[2,12,96,1536]{3,2,1,0:T(8,128)(2,1)} %param.14) | data formatting | bytes 14155776 | tf_op args[2]
  228.0 31.3 %fusion.78 = (f32[24,48,96]{2,1,0:T(8,128)S(1)}, f32[24,48,96,96]{2,3,1,0:T(8,128)}) fusion(f32[48,96,96]{1,2,0:T(8,128)S(1)} %bitcast.92, bf16[24,96,48,32]{1,3,2,0:T(8,128)(2,1)} %bitcast.86, bf16[24,96,48,32]{1,3,2,0:T(8,128)(2,1)} %bitcast.87), kind=kOutput, calls=%fused_computation.88 | convolution fusion | flops 721944640 | bytes 58834944 | tf_op jit(solution)/shard_map/sub | solution.py:83
  259.3 26.5 %convert_bitcast_fusion = bf16[24,96,48,32]{1,3,2,0:T(8,128)(2,1)} fusion(bf16[24,96,48,32]{1,3,2,0:T(8,128)(2,1)} %bitcast.81, f32[24,48,96,96]{2,3,1,0:T(8,128)} %get-tuple-element.31, f32[24,48,96]{2,1,0:T(8,128)S(1)} %get-tuple-element.30), kind=kOutput, calls=%fused_computation.34 | convolution fusion | flops 704249856 | bytes 57065472 | tf_op jit(solution)/shard_map/nhqk,nkhd->nqhd/dot_general | solution.py:85
  285.8 18.2 %copy.128 = bf16[24,96,48,32]{1,0,3,2:T(8,128)(2,1)} copy(bf16[24,96,48,32]{1,3,2,0:T(8,128)(2,1)} %convert_bitcast_fusion) | data formatting | bytes 14155776 | tf_op jit(solution)/shard_map/convert_element_type | solution.py:87
  304.0 15.2 %reshape.125 = bf16[2304,1536]{0,1:T(8,128)(2,1)} reshape(bf16[24,96,48,32]{1,0,3,2:T(8,128)(2,1)} %copy.128) | data formatting | bytes 14155776 | tf_op jit(solution)/shard_map/reshape | solution.py:88
  319.2 38.3 %all-gather.2.cloned.1.call-done = bf16[1536,1536]{1,0:T(8,128)(2,1)} async-done(((bf16[48,1536]{1,0:T(8,128)(2,1)}), bf16[1536,1536]{1,0:T(8,128)(2,1)}) %all-gather.2.cloned.1.call-update) | async-done | bytes 4718608 | tf_op jit(solution)/shard_map/all_gather | solution.py:43
  357.5 14.7 %convolution_convert_fusion.1 = bf16[2304,1536]{1,0:T(8,128)(2,1)S(1)} fusion(bf16[2304,1536]{0,1:T(8,128)(2,1)} %reshape.125, bf16[1536,1536]{1,0:T(8,128)(2,1)} %all-gather.2.cloned.1.call-done), kind=kOutput, calls=%fused_computation.33 | convolution fusion | flops 10875174912 | bytes 18874368 | tf_op jit(solution)/shard_map/dot_general | solution.py:90
  372.2 15.4 %copy.129 = bf16[2,12,96,1536]{3,0,1,2:T(2,128)(2,1)} copy(bf16[2,12,96,1536]{3,2,1,0:T(8,128)(2,1)S(1)} %bitcast.90) | data formatting | bytes 14155776 | tf_op jit(solution)/shard_map/reshape | solution.py:91
  401.0 11.4 %reshape.135 = bf16[2304,1536]{1,0:T(8,128)(2,1)} reshape(bf16[2,12,8,12,1536]{4,3,2,1,0:T(8,128)(2,1)} %copy.142) | data formatting | bytes 14155776 | tf_op jit(solution)/shard_map/reshape | solution.py:121
  412.5 16.6 %convolution_convert_fusion = bf16[2304,1536]{1,0:T(8,128)(2,1)} fusion(bf16[2304,1536]{1,0:T(8,128)(2,1)} %reshape.135, bf16[1536,1536]{1,0:T(8,128)(2,1)} %all-gather.2.cloned.1.call-done), kind=kOutput, calls=%fused_computation.32 | convolution fusion | flops 10875174912 | bytes 18874368 | tf_op jit(solution)/shard_map/dot_general | solution.py:122
  439.2 18.7 %reshape.136 = bf16[24,96,48,32]{1,0,3,2:T(8,128)(2,1)} reshape(bf16[2304,1536]{0,1:T(8,128)(2,1)} %copy.143) | data formatting | bytes 14155776 | tf_op jit(solution)/shard_map/reshape | solution.py:125
  457.9 42.0 %fusion = f32[24,48,96,96]{2,3,1,0:T(8,128)} fusion(bf16[24,96,48,32]{1,3,2,0:T(8,128)(2,1)} %bitcast.82, bf16[24,96,48,32]{1,0,3,2:T(8,128)(2,1)} %reshape.136, f32[24,48,96,96]{2,3,1,0:T(8,128)} %get-tuple-element.31, f32[24,48,96]{2,1,0:T(8,128)S(1)} %get-tuple-element.30), kind=kOutput, calls=%fused_computation | convolution fusion | flops 700821568 | bytes 99532800 | tf_op jit(solution)/shard_map/sub | solution.py:39
  499.9 45.0 %multiply_reduce_fusion = f32[48,96,96]{1,2,0:T(8,128)} fusion(f32[24,48,96,96]{2,3,1,0:T(8,128)} %fusion, f32[24,48,96,96]{2,3,1,0:T(8,128)} %get-tuple-element.31, f32[24,48,96]{2,1,0:T(8,128)S(1)} %get-tuple-element.30, bf16[24,96,48,32]{1,3,2,0:T(8,128)(2,1)} %bitcast.83, bf16[24,96,48,32]{1,0,3,2:T(8,128)(2,1)} %reshape.136), kind=kOutput, calls=%fused_computation.8 | convolution fusion | flops 721502208 | bytes 101302272 | tf_op jit(solution)/shard_map/nqhd,nkhd->nhqk/dot_general | solution.py:126
  558.0 35.1 %reshape.127 = bf16[2,96,12,48,32]{4,3,0,2,1:T(8,128)(2,1)} reshape(bf16[2,8,12,12,1536]{4,0,3,2,1:T(2,128)(2,1)} %copy.131) | data formatting | bytes 14155776 | tf_op jit(solution)/shard_map/reshape | solution.py:95
  593.1 29.4 %copy.135 = bf16[2,96,12,48,32]{1,4,3,2,0:T(8,128)(2,1)} copy(bf16[2,96,12,48,32]{4,3,0,2,1:T(8,128)(2,1)} %reshape.127) | data formatting | bytes 14155776 | tf_op jit(solution)/shard_map/reshape | solution.py:95
  622.5 25.4 %fusion.80 = f32[2,12,48,96,96]{4,3,2,1,0:T(8,128)} fusion(bf16[2,96,12,48,32]{1,4,3,2,0:T(8,128)(2,1)} %copy.135, bf16[2,96,12,48,32]{1,4,3,2,0:T(8,128)(2,1)} %bitcast.79), kind=kOutput, calls=%fused_computation.90 | convolution fusion | flops 679477248 | bytes 56623104 | tf_op jit(solution)/shard_map/bqchd,bkchd->bchqk/dot_general | solution.py:109
  647.9 60.8 %fusion.5 = f32[48,96,96]{1,2,0:T(8,128)} fusion(f32[2,12,48,96,96]{4,3,2,1,0:T(8,128)} %fusion.80, f32[2,12,48,96,96]{3,4,2,1,0:T(8,128)} %get-tuple-element.33, f32[2,12,48,96]{3,2,1,0:T(8,128)S(1)} %copy-done.15, bf16[2,96,12,48,32]{1,4,3,2,0:T(8,128)(2,1)} %copy.135, bf16[2,96,12,48,32]{1,4,3,2,0:T(8,128)(2,1)} %bitcast.80), kind=kOutput, calls=%fused_computation.7 | convolution fusion | flops 742846528 | bytes 101302272 | tf_op jit(solution)/shard_map/sub | solution.py:39
  723.9 41.3 %psum.24 = f32[191,48]{0,1:T(8,128)S(1)} all-reduce(f32[191,48]{0,1:T(8,128)S(1)} %fusion.46), channel_id=1, replica_groups=mesh['dp'=4,'grid'=8] {'dp','grid'}, use_global_device_ids=true, to_apply=%region_7.0 | all-reduce | flops 9168 | bytes 73344 | tf_op jit(solution)/shard_map/psum | solution.py:114
  767.0 26.0 %fusion.34 = bf16[2,12,48,32,96]{4,3,2,1,0:T(8,128)(2,1)} fusion(bf16[2,96,12,48,32]{1,4,3,2,0:T(8,128)(2,1)} %copy.135, f32[2,12,48,96,96]{3,4,2,1,0:T(8,128)} %get-tuple-element.33, f32[2,12,48,96]{3,2,1,0:T(8,128)S(1)} %copy-done.15), kind=kOutput, calls=%fused_computation.44 | convolution fusion | flops 704249856 | bytes 57065472 | tf_op jit(solution)/shard_map/bchqk,bkchd->bqchd/dot_general | solution.py:104
  (66 shorter events, 137.4 us)
Async XLA Ops:
  7.2 0.7 copy-start
  7.2 0.6 copy-start.12
  48.1 136.4 %copy-start.3 = (f32[191,48]{0,1:T(8,128)}, f32[191,48]{0,1:T(8,128)S(1)}, u32[]{:S(2)}) copy-start(f32[191,48]{0,1:T(8,128)S(1)} %psum.21) | copy-start | bytes 110020
  49.1 0.6 copy-start.5
  81.0 11.5 %copy-start.1 = (f32[96,96,48]{0,1,2:T(8,128)S(1)}, f32[96,96,48]{0,1,2:T(8,128)}, u32[]{:S(2)}) copy-start(f32[96,96,48]{0,1,2:T(8,128)} %copy.134) | copy-start | bytes 5308420
  123.8 37.6 %copy-start.14 = (f32[2,12,48,96]{3,2,1,0:T(8,128)}, f32[2,12,48,96]{3,2,1,0:T(8,128)S(1)}, u32[]{:S(2)}) copy-start(f32[2,12,48,96]{3,2,1,0:T(8,128)S(1)} %get-tuple-element.32) | copy-start | bytes 1327108
  178.7 5.7 copy-start.9
  178.7 208.9 %all-to-all-start.1 = ((bf16[2,96,12,1536]{3,0,2,1:T(2,128)(2,1)}), bf16[2,96,12,1536]{3,0,2,1:T(2,128)(2,1)}, u32[]{:S(2)}, u32[]{:S(2)}) async-start(bf16[2,96,12,1536]{3,0,2,1:T(2,128)(2,1)} %copy.141), calls=%async_computation.1 | async-start | bytes 14155776 | tf_op jit(solution)/shard_map/all_to_all | solution.py:120
  183.6 173.8 %all-gather.2.cloned.1.call-start = ((), (), s32[]{:S(2)}) async-start(), calls=%async_computation.2 | async-start | bytes 4866048 | tf_op jit(solution)/shard_map/all_gather | solution.py:43
  184.6 0.6 copy-start.7
  216.6 11.5 %copy-start.2 = (f32[96,96,48]{0,1,2:T(8,128)S(1)}, f32[96,96,48]{0,1,2:T(8,128)}, u32[]{:S(2)}) copy-start(f32[96,96,48]{0,1,2:T(8,128)} %copy.125) | copy-start | bytes 5308420
  387.6 161.9 %all-to-all-start = ((bf16[2,12,96,1536]{3,0,1,2:T(2,128)(2,1)}), bf16[2,12,96,1536]{3,0,1,2:T(2,128)(2,1)}, u32[]{:S(2)}, u32[]{:S(2)}) async-start(bf16[2,12,96,1536]{3,0,1,2:T(2,128)(2,1)} %copy.129), calls=%async_computation | async-start | bytes 14155776 | tf_op jit(solution)/shard_map/all_to_all | solution.py:92
  622.5 25.4 %copy-start.15 = (f32[2,12,48,96]{3,2,1,0:T(8,128)S(1)}, f32[2,12,48,96]{3,2,1,0:T(8,128)}, u32[]{:S(2)}) copy-start(f32[2,12,48,96]{3,2,1,0:T(8,128)} %copy-done.14) | copy-start | bytes 1327108
  647.9 65.5 %copy-start.6 = (s32[9216]{0:T(1024)S(1)}, s32[9216]{0:T(1024)}, u32[]{:S(2)}) copy-start(s32[9216]{0:T(1024)} %copy-done.5) | copy-start | bytes 110596
  708.6 9.9 %copy-start.8 = (s32[9216]{0:T(1024)S(1)}, s32[9216]{0:T(1024)}, u32[]{:S(2)}) copy-start(s32[9216]{0:T(1024)} %copy-done.7) | copy-start | bytes 110596
  708.6 56.6 %copy-start.4 = (f32[191,48]{0,1:T(8,128)S(1)}, f32[191,48]{0,1:T(8,128)}, u32[]{:S(2)}) copy-start(f32[191,48]{0,1:T(8,128)} %copy-done.3) | copy-start | bytes 110020
  708.7 56.6 %copy-start.10 = (f32[64]{0:T(128)S(1)}, f32[64]{0:T(128)}, u32[]{:S(2)}) copy-start(f32[64]{0:T(128)} %param.22) | copy-start | bytes 772
  708.7 56.6 %copy-start.11 = (f32[64]{0:T(128)S(1)}, f32[64]{0:T(128)}, u32[]{:S(2)}) copy-start(f32[64]{0:T(128)} %param.21) | copy-start | bytes 772
  708.7 56.6 %copy-start.13 = (f32[191]{0:T(256)S(1)}, f32[191]{0:T(256)}, u32[]{:S(2)}) copy-start(f32[191]{0:T(256)} %copy-done.12) | copy-start | bytes 2296
Sparse Core Ops, SparseCore 0:
  187.4 170.0 all-gather.1
where the time goes:
time: 820 us; the launch traced here: 811 us
  matrix products  379 us (46%)
  local copies, waits for them, and re-layouts  287 us (35%)
  blocking collectives  80.6 us (10%)
  waiting for transfers between devices  39 us (5%)
  between operations  14.5 us (2%)
  starting transfers between devices  9.84 us (1%)
    sub x2, matrix products, soft_grad(): d_probs - jnp.sum(attn_probs * d_probs, axis=-1, keepdims=True)  103 us
    unnamed x39, local copies, waits for them, and re-layouts  81.7 us
    reshape x2, local copies, waits for them, and re-layouts, shards(): value_cols = col_values.reshape(images, G, col_count, NH, HD)  64.5 us
    dot_general x1, matrix products, shards(): jnp.einsum('nqhd,nkhd->nhqk', d_row_out, value_rows, preferred_element_ty...  45 us
    psum x1, blocking collectives, shards(): col_summed = lax.psum(col_table, ('dp', 'grid'))  41.3 us
    psum x1, blocking collectives, shards(): table_pre = lax.psum(partial_table, 'grid')  39.3 us
    all_gather x1, waiting for transfers between devices, fetch_weight(): return lax.all_gather(w_value, ('dp', 'grid'), axis=0, tiled=True)  38.3 us
    dot_general x1, matrix products, shards(): jnp.einsum('bchqk,bqchd->bkchd', p_col_b, grad_cols, preferred_element_ty...  37.6 us
  transfers between devices with their start and end apart: 3, of which 1 were waited for; matrix products, arithmetic and copies ran while one was open for 40% of the time, Pallas kernels for 0%

commit v1 on v0

v1 whole, which is shorter than its diff:
```python
import functools
import math

import jax
import jax.numpy as jnp
from jax import lax
from jax.experimental import pallas as pl
from jax.experimental.pallas import tpu as pltpu
from jax.sharding import PartitionSpec as P

LANES = 128
F32 = jnp.float32
BF16 = jnp.bfloat16
PRECISE = lax.Precision.HIGHEST


def offset_coords(tokens):
    delta = jnp.arange(2 * tokens - 1, dtype=F32) - (tokens - 1)
    scaled = delta * (8.0 / (tokens - 1))
    return jnp.sign(scaled) * jnp.log2(jnp.abs(scaled) + 1.0) / 3.0


def offset_one_hot(positions, tokens):
    spread = positions[None, :] - positions[:, None] + (tokens - 1)
    levels = jnp.arange(2 * tokens - 1, dtype=jnp.int32)
    return (levels[:, None] == spread.reshape(-1)[None, :]).astype(F32)


def spread_sum(x, axis_name):
    n = lax.axis_size(axis_name)
    copies = jnp.broadcast_to(x[None], (n,) + x.shape)
    return jnp.sum(lax.all_to_all(copies, axis_name, 0, 0), axis=0)


def stacked(x, hd):
    lane = lax.broadcasted_iota(jnp.int32, (1, LANES), 1) // hd
    return jnp.concatenate(
        [x * (lane == h).astype(F32).astype(BF16) for h in range(LANES // hd)], axis=0
    )


def dot(a, b, ca, cb):
    return lax.dot_general(a, b, (((ca,), (cb,)), ((), ())), preferred_element_type=F32)


def probs(k, q_stack, bias, scale):
    s = dot(k, q_stack, 1, 1) * scale + bias
    e = jnp.exp2(s - jnp.max(s, axis=0, keepdims=True))
    return e * (1.0 / jnp.sum(e, axis=0, keepdims=True))


def mix(p, v, hd):
    tokens = v.shape[0]
    full = dot(v, p, 0, 0)
    parts = [
        full[h * hd : (h + 1) * hd, h * tokens : (h + 1) * tokens] for h in range(LANES // hd)
    ]
    return jnp.concatenate(parts, axis=0).T


def soft_grad(p, dp):
    return p * (dp - jnp.sum(p * dp, axis=0, keepdims=True))


def load_bias(bias_ref, bias_s, heads):
    @pl.when(pl.program_id(1) == 0)
    def _():
        bias_s[...] = jnp.concatenate(
            [bias_ref[h] * math.log2(math.e) for h in range(heads)], axis=1
        )


def unpack_columns(ref, scratch, stride):
    tokens, columns = ref.shape[1], ref.shape[2]
    wide = scratch.reshape(tokens, stride, LANES)
    wide[:, 0:columns, :] = ref[0].astype(F32)


def column(scratch, j, tokens, stride):
    return scratch[pl.ds(j, tokens, stride=stride), :]


def pack_columns(ref, scratch, stride):
    tokens, columns = ref.shape[1], ref.shape[2]
    wide = scratch.reshape(tokens, stride, LANES)
    ref[0] = wide[:, 0:columns, :].astype(BF16)


def row_forward(hd, q_ref, k_ref, v_ref, bias_ref, out_ref, p_ref, bias_s):
    load_bias(bias_ref, bias_s, LANES // hd)
    scale = hd**-0.5 * math.log2(math.e)
    for r in range(q_ref.shape[1]):
        p = probs(k_ref[0, r], stacked(q_ref[0, r], hd), bias_s[...], scale).astype(BF16)
        p_ref[0, r, 0] = p
        out_ref[0, r] = mix(p, v_ref[0, r], hd).astype(BF16)


def fold_out(acc, ds_ref, heads):
    @pl.when(pl.program_id(1) == pl.num_programs(1) - 1)
    def _():
        tokens = ds_ref.shape[1]
        for h in range(heads):
            ds_ref[h] = acc[:, h * tokens : (h + 1) * tokens]


def start_acc(acc):
    @pl.when(pl.program_id(1) == 0)
    def _():
        acc[...] = jnp.zeros_like(acc)


def row_backward(hd, p_ref, v_ref, d_ref, ds_ref, acc):
    start_acc(acc)
    for r in range(v_ref.shape[1]):
        dp = dot(v_ref[0, r], stacked(d_ref[0, r], hd), 1, 1)
        acc[...] += soft_grad(p_ref[0, r, 0].astype(F32), dp)
    fold_out(acc, ds_ref, LANES // hd)


def col_forward(hd, stride, q_ref, k_ref, c_ref, bias_ref, dv_ref, p_ref, bias_s, qs, ks, cs, os):
    load_bias(bias_ref, bias_s, LANES // hd)
    scale = hd**-0.5 * math.log2(math.e)
    tokens, columns = q_ref.shape[1], q_ref.shape[2]
    for ref, scratch in ((q_ref, qs), (k_ref, ks), (c_ref, cs)):
        unpack_columns(ref, scratch, stride)
    for j in range(columns):
        q, k, c = (column(s, j, tokens, stride).astype(BF16) for s in (qs, ks, cs))
        p = probs(k, stacked(q, hd), bias_s[...], scale).astype(BF16)
        p_ref[0, j, 0] = p
        os[pl.ds(j, tokens, stride=stride), :] = dot(p, stacked(c, hd), 1, 0)
    pack_columns(dv_ref, os, stride)


def col_backward(hd, stride, p_ref, v_ref, c_ref, out_ref, ds_ref, acc, vs, cs, os):
    start_acc(acc)
    tokens, columns = v_ref.shape[1], v_ref.shape[2]
    for ref, scratch in ((v_ref, vs), (c_ref, cs)):
        unpack_columns(ref, scratch, stride)
    for j in range(columns):
        v, c = (column(s, j, tokens, stride).astype(BF16) for s in (vs, cs))
        p = p_ref[0, j, 0]
        os[pl.ds(j, tokens, stride=stride), :] = mix(p, v, hd)
        dp = dot(v, stacked(c, hd), 1, 1)
        acc[...] += soft_grad(p.astype(F32), dp)
    pack_columns(out_ref, os, stride)
    fold_out(acc, ds_ref, LANES // hd)


def shards(
    q_row,
    k_row,
    v_row,
    q_col,
    k_col,
    cotangent,
    w_value,
    row_positions,
    col_positions,
    mlp_in,
    mlp_bias,
    mlp_out,
):
    images, row_count, tokens, width = q_row.shape
    col_count = q_col.shape[2]
    n_heads = mlp_out.shape[1]
    hd = width // n_heads
    heads = LANES // hd
    chunks = width // LANES
    wide = heads * tokens
    stride = -(-col_count // 8) * 8
    n_off = 2 * tokens - 1

    whole_weight = lax.all_gather(w_value, ("dp", "grid"), axis=0, tiled=True)

    coords = offset_coords(tokens)
    pre_act = coords[:, None] * mlp_in[None, :] + mlp_bias[None, :]
    hidden_units = jnp.maximum(pre_act, 0.0)
    partial_table = lax.dot_general(
        mlp_out, hidden_units, (((0,), (1,)), ((), ())), precision=PRECISE
    )
    squashed = jax.nn.sigmoid(spread_sum(partial_table, "grid"))
    bias_table = 16.0 * squashed
    hot_cols = offset_one_hot(col_positions, tokens)
    hot_rows = offset_one_hot(row_positions, tokens)
    bias_row = jnp.dot(bias_table, hot_cols, precision=PRECISE).reshape(n_heads, tokens, tokens)
    bias_col = jnp.dot(bias_table, hot_rows, precision=PRECISE).reshape(n_heads, tokens, tokens)

    row_block = pl.BlockSpec((1, row_count, tokens, LANES), lambda c, n: (n, 0, 0, c))
    col_block = pl.BlockSpec((1, tokens, col_count, LANES), lambda c, n: (n, 0, 0, c))
    head_block = pl.BlockSpec((heads, tokens, tokens), lambda c, n: (c, 0, 0))
    row_p_block = pl.BlockSpec((1, row_count, 1, tokens, wide), lambda c, n: (n, 0, c, 0, 0))
    col_p_block = pl.BlockSpec((1, col_count, 1, tokens, wide), lambda c, n: (n, 0, c, 0, 0))
    row_shape = jax.ShapeDtypeStruct((images, row_count, tokens, width), BF16)
    col_shape = jax.ShapeDtypeStruct((images, tokens, col_count, width), BF16)
    row_p_shape = jax.ShapeDtypeStruct((images, row_count, chunks, tokens, wide), BF16)
    col_p_shape = jax.ShapeDtypeStruct((images, col_count, chunks, tokens, wide), BF16)
    sums_shape = jax.ShapeDtypeStruct((n_heads, tokens, tokens), F32)
    square = pltpu.VMEM((tokens, wide), F32)
    column_scratch = pltpu.VMEM((tokens * stride, LANES), F32)
    grid = (chunks, images)
    params = pltpu.CompilerParams(vmem_limit_bytes=56 * 1024 * 1024)
    cost = pl.CostEstimate(
        flops=40 * 2**30, bytes_accessed=60 * 2**20, transcendentals=20 * 2**20
    )

    def call(body, in_specs, out_specs, out_shape, scratch, name):
        return pl.pallas_call(
            body,
            grid=grid,
            in_specs=in_specs,
            out_specs=out_specs,
            out_shape=out_shape,
            scratch_shapes=scratch,
            compiler_params=params,
            cost_estimate=cost,
            name=name,
        )

    d_values, p_col = call(
        functools.partial(col_forward, hd, stride),
        [col_block, col_block, col_block, head_block],
        [col_block, col_p_block],
        [col_shape, col_p_shape],
        [square] + [column_scratch] * 4,
        "col_forward",
    )(q_col, k_col, cotangent, bias_col)
    d_rows = lax.all_to_all(d_values, "grid", split_axis=1, concat_axis=2, tiled=True)

    row_out, p_row = call(
        functools.partial(row_forward, hd),
        [row_block, row_block, row_block, head_block],
        [row_block, row_p_block],
        [row_shape, row_p_shape],
        [square],
        "row_forward",
    )(q_row, k_row, v_row, bias_row)
    flat_out = row_out.reshape(images * row_count * tokens, width)
    values = jnp.dot(flat_out, whole_weight, preferred_element_type=F32).astype(BF16)
    values = values.reshape(images, row_count, tokens, width)
    col_values = lax.all_to_all(values, "grid", split_axis=2, concat_axis=1, tiled=True)

    flat_grad = d_rows.reshape(images * row_count * tokens, width)
    d_row_out = dot(flat_grad, whole_weight, 1, 1).astype(BF16)
    d_row_out = d_row_out.reshape(images, row_count, tokens, width)
    row_sums = call(
        functools.partial(row_backward, hd),
        [row_p_block, row_block, row_block],
        head_block,
        sums_shape,
        [square],
        "row_backward",
    )(p_row, v_row, d_row_out)

    attended, col_sums = call(
        functools.partial(col_backward, hd, stride),
        [col_p_block, col_block, col_block],
        [col_block, head_block],
        [col_shape, sums_shape],
        [square] + [column_scratch] * 3,
        "col_backward",
    )(p_col, col_values, cotangent)

    def fold(sums, hot):
        flat = sums.reshape(n_heads, tokens * tokens)
        return lax.dot_general(flat, hot, (((1,), (1,)), ((), ())), precision=PRECISE)

    table = fold(row_sums, hot_cols) + fold(col_sums, hot_rows)
    table_sum = spread_sum(spread_sum(table, "grid"), "dp")
    batch_size = lax.axis_size("dp") * images
    table_grad = table_sum / (batch_size * tokens)
    pre_grad = table_grad * 16.0 * squashed * (1.0 - squashed)
    grad_mlp_out = lax.dot_general(
        hidden_units, pre_grad, (((0,), (1,)), ((), ())), precision=PRECISE
    )
    back_units = lax.dot_general(pre_grad, mlp_out, (((0,), (1,)), ((), ())), precision=PRECISE)
    unit_grad = jnp.where(pre_act > 0, back_units, 0.0)
    grad_mlp_in = jnp.sum(unit_grad * coords[:, None], axis=0)
    grad_mlp_bias = jnp.sum(unit_grad, axis=0)
    return (attended, grad_mlp_in, grad_mlp_bias, grad_mlp_out)


def solution(mesh):
    return jax.shard_map(
        shards,
        mesh=mesh,
        in_specs=(
            P("dp", "grid", None, None),
            P("dp", "grid", None, None),
            P("dp", "grid", None, None),
            P("dp", None, "grid", None),
            P("dp", None, "grid", None),
            P("dp", None, "grid", None),
            P(("dp", "grid"), None),
            P(),
            P(),
            P("grid"),
            P("grid"),
            P("grid", None),
        ),
        out_specs=(P("dp", None, "grid", None), P("grid"), P("grid"), P("grid", None)),
        check_vma=False,
    )
```

time: 820 us -> 642 us (0.78)
  matrix products: 379 us -> 46.9 us
  Pallas kernels: 0 us -> 242 us
  local copies, waits for them, and re-layouts: 287 us -> 116 us
  waiting for transfers between devices: 39 us -> 174 us
  blocking collectives: 80.6 us -> 15.7 us
  starting transfers between devices: 9.84 us -> 21.9 us
    pallas_call x0 -> x4, Pallas kernels: none -> 242 us  [the longest x1 90.6 us: shards(): call(functools.partial(row_forward, hd), [row_block, row_block, row_block...]
    dot_general x14 -> x9, matrix products: 214 us -> 46.9 us  [the longest x1 16.7 us: dot(): lax.dot_general(a, b, (((ca,), (cb,)), ((), ())), preferred_element_type=...]
    sub x4 -> x0, matrix products: 165 us -> none  [the longest x2 103 us: soft_grad(): d_probs - jnp.sum(attn_probs * d_probs, axis=-1, keepdims=True)]
    reshape x13 -> x6, local copies, waits for them, and re-layouts: 156 us -> 37.2 us  [the longest x1 15.4 us: shards(): values = values.reshape(images, row_count, tokens, width)]
    all_to_all x1, waiting for transfers between devices: 0.01 us -> 82.4 us  [shards(): lax.all_to_all(values, 'grid', split_axis=2, concat_axis=1, tiled=True)]
    psum x2 -> x0, blocking collectives: 80.6 us -> none  [the longest x1 41.3 us: shards(): col_summed = lax.psum(col_table, ('dp', 'grid'))]
    all_gather x1, waiting for transfers between devices: 38.3 us -> 90.8 us  [shards(): whole_weight = lax.all_gather(w_value, ('dp', 'grid'), axis=0, tiled=True)]
    unnamed x39 -> x28, local copies, waits for them, and re-layouts: 81.7 us -> 44.1 us
  transfers between devices with their start and end apart: 3 -> 5, of which waited for: 1 -> 2; matrix products, arithmetic and copies ran while one was open for 40% -> 19% of each run, Pallas kernels for 0% -> 19%
where the time goes in v1:
time: 642 us; the launch traced here: 632 us
  Pallas kernels  242 us (38%)
  waiting for transfers between devices  174 us (27%)
  local copies, waits for them, and re-layouts  116 us (18%)
  matrix products  46.9 us (7%)
  starting transfers between devices  21.9 us (3%)
  blocking collectives  15.7 us (2%)
  between operations  14.7 us (2%)
    all_gather x1, waiting for transfers between devices, shards(): whole_weight = lax.all_gather(w_value, ('dp', 'grid'), axis=0, tiled=True)  90.8 us
    pallas_call x1, Pallas kernels, shards(): call(functools.partial(row_forward, hd), [row_block, row_block, row_block...  90.6 us
    all_to_all x1, waiting for transfers between devices, shards(): lax.all_to_all(values, 'grid', split_axis=2, concat_axis=1, tiled=True)  82.4 us
    pallas_call x1, Pallas kernels, shards(): call(functools.partial(col_forward, hd, stride), [col_block, col_block, c...  78 us
    unnamed x28, local copies, waits for them, and re-layouts  44.1 us
    pallas_call x1, Pallas kernels, shards(): call(functools.partial(col_backward, hd, stride), [col_p_block, col_block...  43.7 us
    pallas_call x1, Pallas kernels, shards(): call(functools.partial(row_backward, hd), [row_p_block, row_block, row_bl...  29.7 us
    dot_general x1, matrix products, dot(): lax.dot_general(a, b, (((ca,), (cb,)), ((), ())), preferred_element_type=...  16.7 us
  transfers between devices with their start and end apart: 5, of which 2 were waited for; matrix products, arithmetic and copies ran while one was open for 19% of the time, Pallas kernels for 19%

profile of v1, /device:TPU:0, one launch (start us, length us, event | category | flops | bytes accessed | tf_op | source)
XLA Modules:
  0.0 631.8 jit_solution(6348614183212365226)
XLA Ops:
  9.6 7.3 %all-to-all-start = ((f32[8,48,191]{2,1,0:T(8,128)}), f32[8,48,191]{2,1,0:T(8,128)S(1)}, u32[]{:S(2)}, u32[]{:S(2)}) async-start(f32[8,48,191]{2,1,0:T(8,128)} %broadcast_in_dim.7), calls=%async_computation | async-start | bytes 786432 | tf_op jit(solution)/shard_map/all_to_all | solution.py:32
  17.8 10.8 %copy.41.c_ref = bf16[2,96,12,1536]{3,2,1,0:T(8,128)(2,1)} copy(bf16[2,96,12,1536]{3,1,2,0:T(8,128)(2,1)} %param.17) | data formatting | bytes 14155776 | tf_op args[5]
  28.7 10.9 %copy.39.q_ref = bf16[2,96,12,1536]{3,2,1,0:T(8,128)(2,1)} copy(bf16[2,96,12,1536]{3,1,2,0:T(8,128)(2,1)} %param.15) | data formatting | bytes 14155776 | tf_op args[3]
  39.5 11.1 %copy.40.k_ref = bf16[2,96,12,1536]{3,2,1,0:T(8,128)(2,1)} copy(bf16[2,96,12,1536]{3,1,2,0:T(8,128)(2,1)} %param.16) | data formatting | bytes 14155776 | tf_op args[4]
  55.8 78.0 %col_forward.1 = (bf16[2,96,12,1536]{3,2,1,0:T(8,128)(2,1)}, bf16[2,12,12,96,384]{4,3,2,1,0:T(8,128)(2,1)}) custom-call(bf16[2,96,12,1536]{3,2,1,0:T(8,128)(2,1)} %copy.39.q_ref, bf16[2,96,12,1536]{3,2,1,0:T(8,128)(2,1)} %copy.40.k_ref, bf16[2,96,12,1536]{3,2,1,0:T(8,128)(2,1)} %copy.41.c_ref, f32[48,96,96]{2,1,0:T(8,128)} %reshape.88.bias_ref), custom_call_target="tpu_custom_call" | custom-call | flops 42949672960 | bytes 62914560 | tf_op jit(solution)/shard_map/col_forward/pallas_call | solution.py:219
  133.7 14.5 %copy.46 = bf16[2,96,12,1536]{3,0,2,1:T(2,128)(2,1)} copy(bf16[2,96,12,1536]{3,2,1,0:T(8,128)(2,1)} %get-tuple-element.14) | data formatting | bytes 14155776 | tf_op jit(solution)/shard_map/col_forward/pallas_call | solution.py:219
  148.2 6.1 all-to-all-start.2
  160.5 90.6 %row_forward.1 = (bf16[2,12,96,1536]{3,2,1,0:T(8,128)(2,1)}, bf16[2,12,12,96,384]{4,3,2,1,0:T(8,128)(2,1)}) custom-call(bf16[2,12,96,1536]{3,2,1,0:T(8,128)(2,1)} %q_ref.2, bf16[2,12,96,1536]{3,2,1,0:T(8,128)(2,1)} %k_ref.2, bf16[2,12,96,1536]{3,2,1,0:T(8,128)(2,1)} %v_ref.3, f32[48,96,96]{2,1,0:T(8,128)} %reshape.89.bias_ref), custom_call_target="tpu_custom_call" | custom-call | flops 42949672960 | bytes 62914560 | tf_op jit(solution)/shard_map/row_forward/pallas_call | solution.py:229
  251.1 90.8 %all-gather.2.cloned.1.call-done = bf16[1536,1536]{1,0:T(8,128)(2,1)} async-done(((bf16[48,1536]{1,0:T(8,128)(2,1)}), bf16[1536,1536]{1,0:T(8,128)(2,1)}) %all-gather.2.cloned.1.call-update) | async-done | bytes 4718608 | tf_op jit(solution)/shard_map/all_gather | solution.py:173
  341.9 14.5 %convolution_convert_fusion.1 = bf16[2304,1536]{1,0:T(8,128)(2,1)S(1)} fusion(bf16[2304,1536]{1,0:T(8,128)(2,1)} %bitcast.24, bf16[1536,1536]{1,0:T(8,128)(2,1)} %all-gather.2.cloned.1.call-done), kind=kOutput, calls=%fused_computation.1 | convolution fusion | flops 10875174912 | bytes 18874368 | tf_op jit(solution)/shard_map/dot_general | solution.py:238
  356.4 15.4 %copy.42 = bf16[2,12,96,1536]{3,0,1,2:T(2,128)(2,1)} copy(bf16[2,12,96,1536]{3,2,1,0:T(8,128)(2,1)S(1)} %bitcast.23) | data formatting | bytes 14155776 | tf_op jit(solution)/shard_map/reshape | solution.py:239
  371.7 4.8 all-to-all-start.1
  376.5 8.7 %copy.51 = bf16[2,8,12,12,1536]{4,3,1,2,0:T(8,128)(2,1)} copy(bf16[2,8,12,12,1536]{4,0,3,2,1:T(2,128)(2,1)} %bitcast.7) | data formatting | bytes 14155776 | tf_op jit(solution)/shard_map/all_to_all | solution.py:227
  385.3 11.4 %reshape.92 = bf16[2304,1536]{1,0:T(8,128)(2,1)} reshape(bf16[2,12,8,12,1536]{4,3,2,1,0:T(8,128)(2,1)} %bitcast.21) | data formatting | bytes 14155776 | tf_op jit(solution)/shard_map/reshape | solution.py:242
  396.7 16.7 %convolution_convert_fusion = bf16[2304,1536]{1,0:T(8,128)(2,1)} fusion(bf16[2304,1536]{1,0:T(8,128)(2,1)} %reshape.92, bf16[1536,1536]{1,0:T(8,128)(2,1)} %all-gather.2.cloned.1.call-done), kind=kOutput, calls=%fused_computation | convolution fusion | flops 10875174912 | bytes 18874368 | tf_op jit(solution)/shard_map/dot_general | solution.py:43
  413.4 29.7 %row_backward.1 = f32[48,96,96]{2,1,0:T(8,128)} custom-call(bf16[2,12,12,96,384]{4,3,2,1,0:T(8,128)(2,1)} %get-tuple-element.13.p_ref, bf16[2,12,96,1536]{3,2,1,0:T(8,128)(2,1)} %v_ref.3, bf16[2,12,96,1536]{3,2,1,0:T(8,128)(2,1)} %bitcast.25), custom_call_target="tpu_custom_call" | custom-call | flops 42949672960 | bytes 62914560 | tf_op jit(solution)/shard_map/row_backward/pallas_call | solution.py:245
  446.1 3.8 fusion
  449.8 82.4 %all-to-all-done.1 = bf16[2,12,96,1536]{3,0,1,2:T(2,128)(2,1)} async-done(((bf16[2,12,96,1536]{3,0,1,2:T(2,128)(2,1)}), bf16[2,12,96,1536]{3,0,1,2:T(2,128)(2,1)}, u32[]{:S(2)}, u32[]{:S(2)}) %all-to-all-start.1) | async-done | bytes 7077920 | tf_op jit(solution)/shard_map/all_to_all | solution.py:240
  532.2 9.5 %copy.44 = bf16[2,8,12,12,1536]{4,3,2,1,0:T(8,128)(2,1)} copy(bf16[2,8,12,12,1536]{4,0,2,3,1:T(2,128)(2,1)} %bitcast.5) | data formatting | bytes 14155776 | tf_op jit(solution)/shard_map/all_to_all | solution.py:240
  541.8 43.7 %col_backward.1 = (bf16[2,96,12,1536]{3,2,1,0:T(8,128)(2,1)}, f32[48,96,96]{2,1,0:T(8,128)}) custom-call(bf16[2,12,12,96,384]{4,3,2,1,0:T(8,128)(2,1)} %get-tuple-element.10.p_ref, bf16[2,96,12,1536]{3,2,1,0:T(8,128)(2,1)} %bitcast.22, bf16[2,96,12,1536]{3,2,1,0:T(8,128)(2,1)} %copy.41.c_ref), custom_call_target="tpu_custom_call" | custom-call | flops 42949672960 | bytes 62914560 | tf_op jit(solution)/shard_map/col_backward/pallas_call | solution.py:254
  588.2 3.8 fusion.8
  592.0 15.7 %all_to_all.48 = f32[8,48,191]{2,1,0:T(8,128)S(1)} all-to-all(f32[8,48,191]{2,1,0:T(8,128)S(1)} %broadcast_in_dim.8), channel_id=1, replica_groups=mesh['dp'=4,'grid'=8] {'grid'}, dimensions={0} | all-to-all | bytes 586752 | tf_op jit(solution)/shard_map/all_to_all | solution.py:32
  608.5 3.6 all-to-all-start.4
  612.1 10.6 %copy.48 = bf16[2,96,12,1536]{3,1,2,0:T(8,128)(2,1)} copy(bf16[2,96,12,1536]{3,2,1,0:T(8,128)(2,1)} %get-tuple-element.28) | data formatting | bytes 14155776
  (49 shorter events, 22.8 us)
Async XLA Ops:
  7.2 0.7 copy-start
  7.2 0.6 copy-start.10
  9.6 41.0 %all-to-all-start = ((f32[8,48,191]{2,1,0:T(8,128)}), f32[8,48,191]{2,1,0:T(8,128)S(1)}, u32[]{:S(2)}, u32[]{:S(2)}) async-start(f32[8,48,191]{2,1,0:T(8,128)} %broadcast_in_dim.7), calls=%async_computation | async-start | bytes 786432 | tf_op jit(solution)/shard_map/all_to_all | solution.py:32
  17.8 32.8 %copy-start.3 = (s32[9216]{0:T(1024)}, s32[9216]{0:T(1024)S(1)}, u32[]{:S(2)}) copy-start(s32[9216]{0:T(1024)S(1)} %add.57) | copy-start | bytes 110596
  50.6 104.7 %copy-start.1 = (f32[48,191]{1,0:T(8,128)}, f32[48,191]{1,0:T(8,128)S(1)}, u32[]{:S(2)}) copy-start(f32[48,191]{1,0:T(8,128)S(1)} %reduce_sum.45) | copy-start | bytes 110020
  148.2 6.9 %copy-start.7 = (s32[96]{0:T(128)S(1)}, s32[96]{0:T(128)}, u32[]{:S(2)}) copy-start(s32[96]{0:T(128)} %param.20) | copy-start | bytes 1156
  148.2 223.5 %all-to-all-start.2 = ((bf16[2,96,12,1536]{3,0,2,1:T(2,128)(2,1)}), bf16[2,96,12,1536]{3,0,2,1:T(2,128)(2,1)}, u32[]{:S(2)}, u32[]{:S(2)}) async-start(bf16[2,96,12,1536]{3,0,2,1:T(2,128)(2,1)} %copy.46), calls=%async_computation.2 | async-start | bytes 14155776 | tf_op jit(solution)/shard_map/all_to_all | solution.py:227
  154.4 187.5 %all-gather.2.cloned.1.call-start = ((), (), s32[]{:S(2)}) async-start(), calls=%async_computation.5 | async-start | bytes 4866048 | tf_op jit(solution)/shard_map/all_gather | solution.py:173
  155.3 95.8 %copy-start.5 = (s32[9216]{0:T(1024)}, s32[9216]{0:T(1024)S(1)}, u32[]{:S(2)}) copy-start(s32[9216]{0:T(1024)S(1)} %add.59) | copy-start | bytes 110596
  371.7 160.5 %all-to-all-start.1 = ((bf16[2,12,96,1536]{3,0,1,2:T(2,128)(2,1)}), bf16[2,12,96,1536]{3,0,1,2:T(2,128)(2,1)}, u32[]{:S(2)}, u32[]{:S(2)}) async-start(bf16[2,12,96,1536]{3,0,1,2:T(2,128)(2,1)} %copy.42), calls=%async_computation.1 | async-start | bytes 14155776 | tf_op jit(solution)/shard_map/all_to_all | solution.py:240
  413.3 32.7 %copy-start.6 = (s32[9216]{0:T(1024)S(1)}, s32[9216]{0:T(1024)}, u32[]{:S(2)}) copy-start(s32[9216]{0:T(1024)} %copy-done.5) | copy-start | bytes 110596
  541.8 46.4 %copy-start.4 = (s32[9216]{0:T(1024)S(1)}, s32[9216]{0:T(1024)}, u32[]{:S(2)}) copy-start(s32[9216]{0:T(1024)} %copy-done.3) | copy-start | bytes 110596
  608.5 14.3 %all-to-all-start.4 = ((f32[4,48,191]{2,1,0:T(8,128)}), f32[4,48,191]{2,1,0:T(8,128)S(1)}, u32[]{:S(2)}, u32[]{:S(2)}) async-start(f32[4,48,191]{2,1,0:T(8,128)} %broadcast_in_dim.9), calls=%async_computation.4 | async-start | bytes 393216 | tf_op jit(solution)/shard_map/all_to_all | solution.py:32
  612.1 10.6 %copy-start.2 = (f32[48,191]{1,0:T(8,128)S(1)}, f32[48,191]{1,0:T(8,128)}, u32[]{:S(2)}) copy-start(f32[48,191]{1,0:T(8,128)} %copy-done.1) | copy-start | bytes 110020
  612.1 10.6 %copy-start.8 = (f32[64]{0:T(128)S(1)}, f32[64]{0:T(128)}, u32[]{:S(2)}) copy-start(f32[64]{0:T(128)} %param.22) | copy-start | bytes 772
  612.1 10.6 %copy-start.9 = (f32[64]{0:T(128)S(1)}, f32[64]{0:T(128)}, u32[]{:S(2)}) copy-start(f32[64]{0:T(128)} %param.21) | copy-start | bytes 772
  612.1 10.6 %copy-start.11 = (f32[191]{0:T(256)S(1)}, f32[191]{0:T(256)}, u32[]{:S(2)}) copy-start(f32[191]{0:T(256)} %copy-done.10) | copy-start | bytes 2296
Sparse Core Ops, SparseCore 0:
  158.1 183.6 all-gather.1
